TPU v7x, 128 devices: a whole 4x4x4 slice. The times are simulated.
128 devices in a mesh: lat: 8 (over x_hi, z), lon: 16 (over y, x_lo, core).
Axes of the slice: x: 4 (x_hi: 2, x_lo: 2; x = x_hi * 2 + x_lo), y: 4, z: 4, core: 2. Of those that a mesh axis runs over, the one named last changes fastest.
Arguments:
- tokens: bfloat16 [2, 128, 384, 1024], P(None, 'lat', 'lon'), may hold values from -6 to 6
- qkv_weight: bfloat16 [1024, 3072], replicated, may hold values from -0.1875 to 0.1875
- out_weight: bfloat16 [1024, 1024], replicated, may hold values from -0.1875 to 0.1875
- merge_weight: bfloat16 [4096, 1024], replicated, may hold values from -0.09375 to 0.09375
- merged_grad: bfloat16 [2, 64, 192, 1024], P(None, 'lat', 'lon'), may hold values from -6 to 6
Outputs:
- merged: bfloat16 [2, 64, 192, 1024], P(None, 'lat', 'lon')
- tokens_grad: bfloat16 [2, 128, 384, 1024], P(None, 'lat', 'lon')
- qkv_weight_grad: float32 [1024, 3072], P(('lat', 'lon'))
- out_weight_grad: float32 [1024, 1024], P(('lat', 'lon'))
All inputs are finite; a program needn't handle non-finite values.
Results may differ from a plain program's by a relative error of at most 0.02.
Values may be sent and summed in bfloat16 or wider, within the bound.
A program may use at most 192 MiB of HBM per device.

v0:
```python
import jax
import jax.numpy as jnp
import numpy as np
from jax import lax
from jax.experimental import pallas as pl
from jax.experimental.pallas import tpu as pltpu
from jax.sharding import PartitionSpec as P

CHUNKS = 4
MESH = pl.DeviceIdType.MESH
F32, BF16 = jnp.float32, jnp.bfloat16
epsilon = 1e-05
SCALE = 32 ** -0.5
MIB = 1024 * 1024
NT = (((1,), (1,)), ((), ()))
TN = (((0,), (0,)), ((), ()))


def dot(left, right, dims=(((1,), (0,)), ((), ()))):
    return lax.dot_general(left, right, dims, preferred_element_type=F32)


def picks(index):
    return (index[:, None] == np.arange(len(index))[None, :]).astype(np.float32)


def window_order():
    t = np.arange(128)
    quarter, level, a, b = t // 32, t // 16 % 2, t // 4 % 4, t % 4
    return picks((level * 8 + 2 * a + quarter % 2) * 8 + 2 * b + quarter // 2)


def orders():
    n = np.arange(128)
    level, i, j = n // 64, n // 8 % 8, n % 8
    to_natural = picks((((i // 4) * 2 + j // 4) * 2 + level) * 16 + (i % 4) * 4 + j % 4)
    to_quarters = window_order() @ to_natural
    n = np.arange(192)
    level, j, i = n // 96, n // 8 % 12, n % 8
    merged_natural = picks((((i // 2) * 6 + j // 2) * 2 + level) * 4 + (i % 2) * 2 + j % 2)
    window, level, a, b = n // 32, n // 16 % 2, n // 4 % 4, n % 4
    row, column = 2 * (window // 3) + a // 2, 2 * (window % 3) + b // 2
    merged_windows = picks(((row * 6 + column) * 2 + level) * 4 + (a % 2) * 2 + b % 2)
    return tuple(jnp.asarray(order, BF16) for order in (to_natural, to_quarters, merged_natural, merged_windows))


def statistics(values):
    center = jnp.mean(values, axis=-1, keepdims=True)
    shifted_values = values - center
    spread = jnp.mean(jnp.square(shifted_values), axis=-1, keepdims=True)
    return shifted_values, lax.rsqrt(spread + epsilon)


def place():
    lat, lon = lax.axis_index("lat"), lax.axis_index("lon")
    return (lat // 4) * 2 + (lon // 2) % 2, lon // 4, lat % 4, lon % 2


def device_at(x, y, z, core):
    return ((x // 2) * 4 + z, y * 4 + (x % 2) * 2 + core)


def neighbours(step):
    lat, lon = lax.axis_index("lat"), lax.axis_index("lon")
    lat_there, lon_there = (lat + step + 8) % 8, (lon + step + 16) % 16
    return (lat_there, lon), (lat, lon_there), (lat_there, lon_there)


def greet(receive_from, send_to):
    barrier = pltpu.get_barrier_semaphore()
    for device in receive_from:
        pl.semaphore_signal(barrier, inc=1, device_id=device, device_id_type=MESH)
    pl.semaphore_wait(barrier, len(send_to))


def remote(source, target, send, recv, device):
    return pltpu.make_async_remote_copy(src_ref=source, dst_ref=target, send_sem=send, recv_sem=recv,
                                        device_id=device, device_id_type=MESH)


def frame_copies(units, first, last, send, recv, base, devices):
    row, column, corner = devices
    return [remote(units.at[first[0], 1:6], units.at[last[0], 1:6], send.at[base], recv.at[base], row),
            remote(units.at[1:4, first[1]], units.at[1:4, last[1]], send.at[base + 1], recv.at[base + 1], column),
            remote(units.at[first[0], first[1]], units.at[last[0], last[1]], send.at[base + 2], recv.at[base + 2], corner)]


def blocks_at(dims, axis, p):
    index = ({"h": p // 2, "l": p % 2}, {"y": p}, {"z": p})[axis]
    return tuple(index.get(dim, slice(None)) for dim in dims)


def left_over(dims, axis):
    return "".join(dim for dim in dims if dim not in ("hl", "y", "z")[axis])


def sizes(dims):
    return tuple({"h": 2, "z": 4, "y": 4, "l": 2}[dim] for dim in dims)


def wide_masks():
    lane = lax.broadcasted_iota(jnp.int32, (128, 256), 1)
    return [lane % 128 // 32 == head for head in range(4)], [lane // 128 == group for group in range(2)]


def stack(values, masks):
    zero = jnp.zeros_like(values)
    return jnp.concatenate([jnp.where(mask, values, zero) for mask in masks], axis=0)


def select(stacked, masks):
    rows = [stacked[128 * head:128 * head + 128] for head in range(4)]
    return jnp.where(masks[0], rows[0], jnp.where(masks[1], rows[1], jnp.where(masks[2], rows[2], rows[3])))


def other_region(rows, columns, edge):
    row = (lax.broadcasted_iota(jnp.int32, (rows, 1), 0) // 4 % 4 < 2) & edge
    column = (lax.broadcasted_iota(jnp.int32, (1, columns), 1) // 4 % 4 < 2) & edge
    return row.astype(jnp.int32) != column.astype(jnp.int32)


def back_kernel(q_hbm, k_hbm, v_hbm, mix_hbm, mix_grad_hbm, normed_hbm, mix_turned_hbm, grad_hbm, x_hbm, weight_hbm,
                merged_in, to_natural, to_quarters, merged_natural, merged_windows,
                qkv_out, out_out, tokens_out, merged_out,
                q, k, v, mix, mix_grad, normed_turned, mix_turned, grad, x_in, qkv_weight,
                dq, dk, dv, g_x, g_y, g_z, g_p, g_r, normed_grad, units, merged_units, *rest):
    stream_buffers, (load, send, recv, strip_send, strip_recv) = rest[:-5], rest[-5:]

    def fetch(index, source, target):
        return pltpu.make_async_copy(source, target, load.at[index])

    def chunk_loads(chunk):
        columns = pl.ds(pl.multiple_of(chunk * 256, 256), 256)
        return [fetch(chunk * 5 + i, source.at[:, columns], target.at[:, columns]) for i, (source, target) in enumerate(
            ((q_hbm, q), (k_hbm, k), (v_hbm, v), (mix_hbm, mix), (mix_grad_hbm, mix_grad)))]

    normed_load, mix_load = fetch(20, normed_hbm, normed_turned), fetch(21, mix_turned_hbm, mix_turned)
    grad_load, weight_load, x_load = fetch(22, grad_hbm, grad), fetch(23, weight_hbm, qkv_weight), fetch(24, x_hbm, x_in)
    mix_load.start()
    grad_load.start()
    for copy in chunk_loads(0):
        copy.start()
    normed_load.start()

    @pl.loop(1, CHUNKS)
    def _(chunk):
        for copy in chunk_loads(chunk):
            copy.start()

    weight_load.start()
    x_load.start()

    x, y, z, core = place()
    here = (x, y, z)

    def moved(axis, step):
        there = list(here)
        there[axis] = (here[axis] + step) % 4
        return device_at(there[0], there[1], there[2], core)

    sibling = device_at(x, y, z, 1 - core)
    ring = [sibling] + [moved(axis, step) for axis in range(3) for step in (1, 2, 3)]
    before, after = neighbours(-1), neighbours(1)
    greet(ring + list(after), ring + list(before))

    units_in = dot(merged_windows[...], merged_in[...], TN).reshape(4, 6, 8, 1024)
    for i in range(4):
        merged_units[i, 0:6] = units_in[i]
    merged_copies = frame_copies(merged_units, (0, 0), (4, 6), strip_send, strip_recv, 0, before)
    for copy in merged_copies:
        copy.start()

    streams = ((g_x, 0), (g_y, 1), (g_z, 2), (g_p, 1), (g_r, 2))
    buffers = tuple(stream_buffers[7 * i:7 * i + 7] for i in range(5))

    def slot_of(kind, chunk):
        return chunk % 2 if kind < 3 else 0

    def core_copy(kind, chunk):
        return remote(streams[kind][0].at[slot_of(kind, chunk), :, 1 - core], buffers[kind][0].at[chunk],
                      send.at[kind, chunk, 0], recv.at[kind, chunk, 0], sibling)

    def level_refs(kind, chunk, level):
        acc = buffers[kind][1 + 2 * level].at[chunk]
        into = buffers[kind][2 + 2 * level].at[chunk]
        dims = "hzyl"
        for i in range(level):
            dims = left_over(dims, (streams[kind][1] + i) % 3)
        return acc, into, dims, (streams[kind][1] + level) % 3

    def level_copies(kind, chunk, level):
        acc, into, dims, axis = level_refs(kind, chunk, level)
        return [remote(acc.at[blocks_at(dims, axis, (here[axis] + i + 1) % 4)], into.at[i],
                       send.at[kind, chunk, 1 + level * 3 + i], recv.at[kind, chunk, 1 + level * 3 + i],
                       moved(axis, i + 1)) for i in range(3)]

    def core_to_first(kind, chunk):
        core_copy(kind, chunk).wait_recv()
        g, (from_core, acc) = streams[kind][0], buffers[kind][:2]
        width = g.shape[-1]

        @pl.loop(0, 8)
        def _(i):
            blocks = pl.ds(i * 8, 8)
            total = g[slot_of(kind, chunk), blocks, core].astype(F32) + from_core[chunk, blocks].astype(F32)
            acc[chunk, i // 4, i % 4] = total.astype(BF16).reshape(4, 2, 16, width)

        for copy in level_copies(kind, chunk, 0):
            copy.start()

    def level_to_next(kind, chunk, level):
        for copy in level_copies(kind, chunk, level):
            copy.wait_recv()
        acc, into, dims, axis = level_refs(kind, chunk, level)
        total = acc[blocks_at(dims, axis, here[axis])].astype(F32)
        for i in range(3):
            total = total + into[i].astype(F32)
        if level < 2:
            buffers[kind][3 + 2 * level][chunk] = total.astype(BF16)
            for copy in level_copies(kind, chunk, level + 1):
                copy.start()
            return
        width = total.shape[-1]
        if kind < 3:
            low = pl.multiple_of(kind * 1024 + chunk * 256, 256)
            qkv_out[:, pl.ds(low, width)] = total[:8]
            qkv_out[:, pl.ds(pl.multiple_of(low + width, 128), width)] = total[8:]
        else:
            low = (kind - 3) * 512
            out_out[:, low:low + width] = total[:8]
            out_out[:, low + width:low + 2 * width] = total[8:]

    head_mask, group_mask = wide_masks()
    row8 = lax.broadcasted_iota(jnp.int32, (8, 256), 0)
    lane8 = lax.broadcasted_iota(jnp.int32, (8, 256), 1) // 32
    own_head = jnp.where(lane8 == row8, 1.0, 0.0).astype(BF16)
    edge = lax.axis_index("lat") == 0
    def put_terms(kind, chunk, i, terms):
        g = streams[kind][0]
        width = g.shape[-1]
        both = jnp.concatenate([terms[:, :, :width], terms[:, :, width:]], axis=1)
        g[slot_of(kind, chunk), pl.ds(i * 16, 16)] = both.astype(BF16).reshape(16, 2, 16, width)

    def window_back(chunk, w):
        columns = pl.ds(pl.multiple_of(chunk * 256, 256), 256)
        rows = pl.ds(pl.multiple_of(w * 128, 128), 128)
        queries, keys, values = q[rows, columns], k[rows, columns], v[rows, columns]
        out_grad = mix_grad[rows, columns]
        product = (out_grad.astype(F32) * mix[rows, columns].astype(F32)).astype(BF16)
        spread_queries, spread_grads = stack(queries, group_mask), stack(out_grad, group_mask)
        weights = jnp.exp(dot(stack(keys, head_mask), spread_queries, NT) * SCALE)
        weights = jnp.where(other_region(512, 256, edge & (w < 3)), 0.0, weights)
        change = dot(stack(values, head_mask), spread_grads, NT)
        means = dot(own_head, product, NT)
        attention, scores_grad = [], []
        for head in range(4):
            part = weights[128 * head:128 * head + 128]
            part = part * (1.0 / jnp.sum(part, axis=0, keepdims=True))
            mean = jnp.concatenate([means[head:head + 1], means[4 + head:5 + head]], axis=1)
            attention.append(part.astype(BF16))
            scores_grad.append((part * (change[128 * head:128 * head + 128] - mean)).astype(BF16))
        dv[rows, columns] = select(dot(jnp.concatenate(attention, axis=0), spread_grads), head_mask).astype(BF16)
        dk[rows, columns] = (select(dot(jnp.concatenate(scores_grad, axis=0), spread_queries), head_mask)
                             * SCALE).astype(BF16)
        turned = keys.T
        pieces = []
        for group in range(2):
            for head in range(4):
                low = group * 128 + head * 32
                pieces.append(dot(turned[low:low + 32], scores_grad[head][:, group * 128:group * 128 + 128]))
        dq[rows, columns] = (jnp.concatenate(pieces, axis=0).T * SCALE).astype(BF16)

    mix_load.wait()
    grad_load.wait()

    @pl.loop(0, 4)
    def _(i):
        rows = pl.ds(pl.multiple_of(i * 256, 256), 256)
        for kind in (3, 4):
            low = (kind - 3) * 512
            put_terms(kind, 0, i, dot(mix_turned[rows], grad[:, low:low + 512]).reshape(32, 8, 512))

    for kind in (3, 4):
        core_copy(kind, 0).start()

    def finish_window(w):
        pieces = []
        for i in range(4):
            rows = pl.ds(pl.multiple_of(w * 128 + i * 32, 32), 32)
            change = normed_grad[rows].astype(BF16).astype(F32)
            centered, inverse = statistics(x_in[rows].astype(F32))
            normed = centered * inverse
            first = jnp.mean(change, axis=-1, keepdims=True)
            second = jnp.mean(change * normed, axis=-1, keepdims=True)
            value = (inverse * (change - first - normed * second)).astype(BF16).astype(F32) + grad[rows].astype(F32)
            pieces.append(value.astype(BF16))
        quarters = dot(to_quarters[...], jnp.concatenate(pieces, axis=0), TN).astype(BF16).reshape(4, 32, 1024)
        wa, wb = w // 3, w % 3
        for u in range(2):
            for side in range(2):
                units[2 * wa + u, 2 * wb + side] = quarters[2 * u + side]

    strips = frame_copies(units, (0, 0), (4, 6), strip_send, strip_recv, 3, before)

    @pl.loop(0, 8)
    def _(t):
        @pl.when(t < CHUNKS)
        def _():
            for copy in chunk_loads(t):
                copy.wait()

            @pl.loop(0, 2)
            def _(wa):
                for wb in range(3):
                    window_back(t, wa * 3 + wb)

        @pl.when((t == 4) | (t == 5))
        def _():
            @pl.when(t == 4)
            def _():
                weight_load.wait()
                x_load.wait()

            tokens = pl.ds(pl.multiple_of((t - 4) * 384, 384), 384)

            @pl.loop(0, 4)
            def _(i):
                rows = pl.ds(pl.multiple_of(i * 256, 256), 256)
                normed_grad[tokens, rows] = (dot(dq[tokens], qkv_weight[rows, 0:1024], NT)
                                             + dot(dk[tokens], qkv_weight[rows, 1024:2048], NT)
                                             + dot(dv[tokens], qkv_weight[rows, 2048:3072], NT))

            @pl.loop(0, 3)
            def _(wb):
                finish_window((t - 4) * 3 + wb)

                @pl.when((t == 5) & (wb == 0))
                def _():
                    strips[1].start()

            @pl.when(t == 4)
            def _():
                strips[0].start()
                strips[2].start()

        @pl.when(t == 6)
        def _():
            for copy in merged_copies:
                copy.wait_recv()
            framed = jnp.concatenate([merged_units[i, 1:7].reshape(48, 1024) for i in range(1, 5)], axis=0)
            merged_out[...] = dot(merged_natural[...], framed.astype(BF16)).astype(BF16)
            strips[1].wait_recv()

        @pl.when(t == 7)
        def _():
            strips[0].wait_recv()
            strips[2].wait_recv()

        @pl.when(t >= 6)
        def _():
            m = t - 6
            blocks = []
            for n in range(3):
                parts = [units[2 * m + 1 + u, 2 * n + 1 + side] for u in range(2) for side in range(2)]
                blocks.append(dot(to_natural[...], jnp.concatenate(parts, axis=0)).reshape(2, 8, 8, 1024))
            tokens_out[:, pl.ds(8 * m, 8)] = jnp.concatenate(blocks, axis=2).astype(BF16)

        for level in (2, 1, 0):
            chunk = t - 2 - level

            @pl.when((chunk >= 0) & (chunk < CHUNKS))
            def _():
                for kind in range(3):
                    level_to_next(kind, chunk, level)

        @pl.when((t >= 1) & (t <= CHUNKS))
        def _():
            for kind in range(3):
                core_to_first(kind, t - 1)

        @pl.when(t == 0)
        def _():
            for kind in (3, 4):
                core_to_first(kind, 0)

            normed_load.wait()

        for level in range(3):
            @pl.when(t == level + 1)
            def _():
                for kind in (3, 4):
                    level_to_next(kind, 0, level)

        @pl.when(t < CHUNKS)
        def _():
            @pl.when(t >= 2)
            def _():
                for kind in range(3):
                    core_copy(kind, t - 2).wait_send()

            columns = pl.ds(pl.multiple_of(t * 256, 256), 256)

            @pl.loop(0, 4)
            def _(i):
                rows = pl.ds(pl.multiple_of(i * 256, 256), 256)
                for kind, right in enumerate((dq, dk, dv)):
                    put_terms(kind, t, i, dot(normed_turned[rows], right[:, columns]).reshape(32, 8, 256))

            for kind in range(3):
                core_copy(kind, t).start()

    for kind in range(3):
        core_copy(kind, 2).wait_send()
        core_copy(kind, 3).wait_send()

    @pl.loop(0, CHUNKS)
    def _(chunk):
        for kind in range(3):
            for level in range(3):
                for copy in level_copies(kind, chunk, level):
                    copy.wait_send()

    for kind in (3, 4):
        core_copy(kind, 0).wait_send()
        for level in range(3):
            for copy in level_copies(kind, 0, level):
                copy.wait_send()
    for copy in merged_copies + strips:
        copy.wait_send()


def back(q, k, v, mix, mix_grad, normed_turned, mix_turned, grad, x, qkv_weight, merged_groups):
    buffers = []
    for axis, count, width in ((0, CHUNKS, 128), (1, CHUNKS, 128), (2, CHUNKS, 128), (1, 1, 256), (2, 1, 256)):
        first = left_over("hzyl", axis)
        second = left_over(first, (axis + 1) % 3)
        for shape in ((64,), (2, 4, 4, 2), (3, *sizes(first)), sizes(first), (3, *sizes(second)), sizes(second), (3,)):
            buffers.append(pltpu.VMEM((count, *shape, 16, width), BF16))
    vmem, anywhere = pl.BlockSpec(memory_space=pltpu.VMEM), pl.BlockSpec(memory_space=pl.ANY)
    tokens = pltpu.VMEM((768, 1024), BF16)
    turned = pltpu.VMEM((1024, 768), BF16)
    return pl.pallas_call(
        back_kernel,
        out_shape=(jax.ShapeDtypeStruct((8, 3072), F32), jax.ShapeDtypeStruct((8, 1024), F32),
                   jax.ShapeDtypeStruct((2, 16, 24, 1024), BF16), jax.ShapeDtypeStruct((192, 1024), BF16)),
        in_specs=[anywhere] * 10 + [vmem] * 5,
        out_specs=(vmem, vmem, vmem, vmem),
        scratch_shapes=[
            tokens, tokens, tokens, tokens, tokens, turned, turned, tokens, tokens, pltpu.VMEM((1024, 3072), BF16),
            tokens, tokens, tokens,
            *[pltpu.VMEM((2, 64, 2, 16, 128), BF16)] * 3, *[pltpu.VMEM((1, 64, 2, 16, 256), BF16)] * 2,
            pltpu.VMEM((768, 1024), F32),
            pltpu.VMEM((5, 7, 32, 1024), BF16),
            pltpu.VMEM((5, 7, 8, 1024), F32),
            *buffers,
            pltpu.SemaphoreType.DMA((25,)),
            pltpu.SemaphoreType.DMA((5, CHUNKS, 10)),
            pltpu.SemaphoreType.DMA((5, CHUNKS, 10)),
            pltpu.SemaphoreType.DMA((6,)),
            pltpu.SemaphoreType.DMA((6,)),
        ],
        compiler_params=pltpu.CompilerParams(collective_id=0, has_side_effects=True, vmem_limit_bytes=62 * MIB),
        name="back",
    )(q, k, v, mix, mix_grad, normed_turned, mix_turned, grad, x, qkv_weight, merged_groups, *orders())


def front_kernel(tokens, merged_grad, weight_hbm, out_weight_hbm, merge_weight_hbm,
                 to_natural, to_quarters, merged_natural, merged_windows,
                 x_hbm, normed_hbm, q_hbm, k_hbm, v_hbm, mix_hbm, mix_turned_hbm, grad_hbm, mix_grad_hbm, merged_out,
                 x, normed, normed_turned, q, k, v, mix, mix_turned, grad, mix_grad,
                 qkv_weight, out_weight, merge_weight, scaled, change, inverses, groups, units, merged_units,
                 load, store, send, recv):
    loads = [pltpu.make_async_copy(source, target, load.at[i]) for i, (source, target) in enumerate(
        ((weight_hbm, qkv_weight), (out_weight_hbm, out_weight), (merge_weight_hbm, merge_weight)))]
    for copy in loads:
        copy.start()
    before, after = neighbours(-1), neighbours(1)
    greet(before, after)
    copies = (frame_copies(units, (4, 6), (0, 0), send, recv, 0, after)
              + frame_copies(merged_units, (4, 6), (0, 0), send, recv, 3, after))

    @pl.loop(0, 32)
    def _(i):
        change[pl.ds(pl.multiple_of(i * 24, 8), 24)] = tokens[i // 16, i % 16].astype(F32)

    @pl.loop(0, 6)
    def _(i):
        m, n = 1 - i // 3, i % 3
        natural = [change[pl.ds(pl.multiple_of((level * 16 + 8 * m + row) * 24 + 8 * n, 8), 8)]
                   for level in range(2) for row in range(8)]
        quarters = dot(to_natural[...], jnp.concatenate(natural, axis=0).astype(BF16), TN)
        quarters = quarters.astype(BF16).reshape(4, 32, 1024)
        for u in range(2):
            for side in range(2):
                units[2 * m + 1 + u, 2 * n + 1 + side] = quarters[2 * u + side]

        @pl.when(i == 2)
        def _():
            copies[0].start()
            copies[2].start()

        @pl.when(i == 5)
        def _():
            copies[1].start()

    merged_in = dot(merged_natural[...], merged_grad[...], TN).reshape(4, 6, 8, 1024)
    for i in range(4):
        merged_units[i + 1, 1:7] = merged_in[i]
    for copy in copies[3:]:
        copy.start()

    def window(w):
        wa, wb = w // 3, w % 3
        quarters = [units[2 * wa + u, 2 * wb + side] for u in range(2) for side in range(2)]
        values = dot(to_quarters[...], jnp.concatenate(quarters, axis=0))
        rows = pl.ds(pl.multiple_of(w * 128, 128), 128)
        x[rows] = values.astype(BF16)
        for i in range(4):
            centered, inverse = statistics(values[32 * i:32 * i + 32])
            normed[pl.ds(pl.multiple_of(w * 128 + 32 * i, 32), 32)] = (centered * inverse).astype(BF16)
        normed_turned[:, rows] = normed[rows].T

    head_mask, group_mask = wide_masks()
    edge = lax.axis_index("lat") == 0

    def project(half, chunk):
        rows = pl.ds(pl.multiple_of(half * 384, 384), 384)
        columns = pl.ds(pl.multiple_of(chunk * 256, 256), 256)
        for third, target in enumerate((q, k, v)):
            low = pl.multiple_of(third * 1024 + chunk * 256, 256)
            target[rows, columns] = dot(normed[rows], qkv_weight[:, pl.ds(low, 256)]).astype(BF16)

    def attend(half, chunk):
        columns = pl.ds(pl.multiple_of(chunk * 256, 256), 256)
        for wb in range(3):
            rows = pl.ds(pl.multiple_of(half * 384 + wb * 128, 128), 128)
            scores = dot(stack(q[rows, columns], head_mask), stack(k[rows, columns], group_mask), NT)
            weights = jnp.exp(scores * SCALE)
            weights = jnp.where(other_region(512, 256, edge & (half == 0)), 0.0, weights)
            pieces = []
            for group in range(2):
                piece = weights[:, group * 128:group * 128 + 128]
                pieces.append((piece * (1.0 / jnp.sum(piece, axis=-1, keepdims=True))).astype(BF16))
            mixture = select(dot(jnp.concatenate(pieces, axis=1), stack(v[rows, columns], group_mask)), head_mask)
            mixture = mixture.astype(BF16)
            mix[rows, columns] = mixture
            mix_turned[columns, rows] = mixture.T

    keeps = [(x, x_hbm), (normed_turned, normed_hbm), (q, q_hbm), (k, k_hbm), (v, v_hbm), (mix, mix_hbm),
             (mix_turned, mix_turned_hbm), (grad, grad_hbm), (mix_grad, mix_grad_hbm)]
    stores = [pltpu.make_async_copy(source, target, store.at[i]) for i, (source, target) in enumerate(keeps)]

    @pl.loop(0, 2)
    def _(phase):
        half = 1 - phase

        @pl.loop(0, 3)
        def _(i):
            @pl.when((phase == 0) & (i == 2))
            def _():
                copies[1].wait_recv()

            @pl.when((phase == 1) & (i == 0))
            def _():
                copies[0].wait_recv()

            @pl.when((phase == 1) & (i == 2))
            def _():
                copies[2].wait_recv()

            window(half * 3 + (i + 1) % 3)

        @pl.when(phase == 0)
        def _():
            loads[0].wait()

        @pl.when(phase == 1)
        def _():
            stores[0].start()
            stores[1].start()

        project(half, 0)

        @pl.loop(0, 3)
        def _(chunk):
            project(half, chunk + 1)
            attend(half, chunk)

        attend(half, 3)

    for copy in stores[2:7]:
        copy.start()
    for copy in copies[3:]:
        copy.wait_recv()
    framed = jnp.concatenate([merged_units[i, 0:6].reshape(48, 1024) for i in range(4)], axis=0)
    groups[...] = dot(merged_windows[...], framed.astype(BF16)).astype(BF16)
    loads[1].wait()

    def add_branch(chunk):
        columns = pl.ds(pl.multiple_of(chunk * 256, 256), 256)
        scaled[:, columns] = x[:, columns].astype(F32) + dot(mix[...], out_weight[:, columns])

    pl.loop(0, 4)(add_branch)

    def quarter_rows(i):
        return [pl.ds(pl.multiple_of(i // 2 * 128 + j * 32 + i % 2 * 16, 16), 16) for j in range(4)]

    def group_rows(i):
        return [pl.ds(pl.multiple_of(j * 192 + i * 16, 16), 16) for j in range(4)]

    def normalize_groups(i):
        parts = [scaled[rows].astype(BF16).astype(F32) for rows in quarter_rows(i)]
        center = sum(jnp.sum(part, axis=-1, keepdims=True) for part in parts) * (1 / 4096)
        parts = [part - center for part in parts]
        spread = sum(jnp.sum(jnp.square(part), axis=-1, keepdims=True) for part in parts) * (1 / 4096)
        inverse = lax.rsqrt(spread + epsilon)
        inverses[pl.ds(pl.multiple_of(i * 16, 16), 16)] = jnp.broadcast_to(inverse, (16, 128))
        for part, rows in zip(parts, group_rows(i)):
            normed[rows] = (part * inverse).astype(BF16)
        for part, rows in zip(parts, quarter_rows(i)):
            scaled[rows] = part * inverse

    pl.loop(0, 12)(normalize_groups)
    loads[2].wait()

    def merge_columns(chunk):
        columns = pl.ds(pl.multiple_of(chunk * 256, 256), 256)
        total = dot(normed[0:192], merge_weight[0:1024, columns])
        for j in range(1, 4):
            total = total + dot(normed[192 * j:192 * j + 192], merge_weight[1024 * j:1024 * j + 1024, columns])
        merged_out[:, columns] = total.astype(BF16)
        for j in range(4):
            rows = pl.ds(pl.multiple_of(j * 1024 + chunk * 256, 256), 256)
            change[192 * j:192 * j + 192, columns] = dot(groups[...], merge_weight[rows], NT)

    pl.loop(0, 4)(merge_columns)

    def group_grads(i):
        changes = [change[rows].astype(BF16).astype(F32) for rows in group_rows(i)]
        values = [scaled[rows] for rows in quarter_rows(i)]
        first = sum(jnp.sum(part, axis=-1, keepdims=True) for part in changes) * (1 / 4096)
        second = sum(jnp.sum(part * value, axis=-1, keepdims=True) for part, value in zip(changes, values)) * (1 / 4096)
        inverse = inverses[pl.ds(pl.multiple_of(i * 16, 16), 16), 0:1]
        for part, value, rows in zip(changes, values, quarter_rows(i)):
            grad[rows] = (inverse * (part - first - value * second)).astype(BF16)

    pl.loop(0, 12)(group_grads)
    stores[7].start()

    def mixture_grads(chunk):
        rows = pl.ds(pl.multiple_of(chunk * 256, 256), 256)
        mix_grad[:, rows] = dot(grad[...], out_weight[rows], NT).astype(BF16)

    pl.loop(0, 4)(mixture_grads)
    stores[8].start()
    for copy in stores:
        copy.wait()
    for copy in copies:
        copy.wait_send()


def front(tokens, merged_grad, qkv_weight, out_weight, merge_weight):
    vmem, anywhere = pl.BlockSpec(memory_space=pltpu.VMEM), pl.BlockSpec(memory_space=pl.ANY)
    rows, turned = jax.ShapeDtypeStruct((768, 1024), BF16), jax.ShapeDtypeStruct((1024, 768), BF16)
    rows_vmem, turned_vmem = pltpu.VMEM((768, 1024), BF16), pltpu.VMEM((1024, 768), BF16)
    return pl.pallas_call(
        front_kernel,
        out_shape=(rows, turned, rows, rows, rows, rows, turned, rows, rows, jax.ShapeDtypeStruct((192, 1024), BF16)),
        in_specs=[vmem] * 2 + [anywhere] * 3 + [vmem] * 4,
        out_specs=(anywhere,) * 9 + (vmem,),
        scratch_shapes=[
            rows_vmem, rows_vmem, turned_vmem, rows_vmem, rows_vmem, rows_vmem, rows_vmem, turned_vmem, rows_vmem,
            rows_vmem,
            pltpu.VMEM((1024, 3072), BF16), pltpu.VMEM((1024, 1024), BF16), pltpu.VMEM((4096, 1024), BF16),
            pltpu.VMEM((768, 1024), F32), pltpu.VMEM((768, 1024), F32), pltpu.VMEM((192, 128), F32),
            pltpu.VMEM((192, 1024), BF16),
            pltpu.VMEM((5, 7, 32, 1024), BF16),
            pltpu.VMEM((5, 7, 8, 1024), F32),
            pltpu.SemaphoreType.DMA((3,)),
            pltpu.SemaphoreType.DMA((9,)),
            pltpu.SemaphoreType.DMA((6,)),
            pltpu.SemaphoreType.DMA((6,)),
        ],
        compiler_params=pltpu.CompilerParams(collective_id=1, has_side_effects=True, vmem_limit_bytes=62 * MIB),
        name="front",
    )(tokens, merged_grad, qkv_weight, out_weight, merge_weight, *orders())


def shards(tokens, qkv_weight, out_weight, merge_weight, merged_grad):
    x, normed_turned, q, k, v, mixture, mix_turned, grad, mixture_grad, merged_groups = front(
        tokens, merged_grad.transpose(0, 2, 1, 3).reshape(192, 1024), qkv_weight, out_weight, merge_weight)
    qkv_weight_grad, out_weight_grad, tokens_grad, merged = back(
        q, k, v, mixture, mixture_grad, normed_turned, mix_turned, grad, x, qkv_weight, merged_groups)
    merged = merged.reshape(2, 12, 8, 1024).transpose(0, 2, 1, 3)
    return (merged, tokens_grad, qkv_weight_grad, out_weight_grad)


def solution(mesh):
    in_specs = (P(None, "lat", "lon", None), P(), P(), P(), P(None, "lat", "lon", None))
    out_specs = (
        P(None, "lat", "lon", None),
        P(None, "lat", "lon", None),
        P(("lat", "lon"), None),
        P(("lat", "lon"), None),
    )
    return jax.shard_map(shards, mesh=mesh, in_specs=in_specs, out_specs=out_specs, check_vma=False)
```

profile of v0, /device:TPU:1, one launch (start us, length us, event | category | flops | bytes accessed | tf_op | source)
XLA Modules:
  0.0 128.8 jit_solution(4617591384646858765)
XLA Ops:
  0.6 46.2 %front.1 = (bf16[768,1024]{1,0:T(8,128)(2,1)}, bf16[1024,768]{1,0:T(8,128)(2,1)}, bf16[768,1024]{1,0:T(8,128)(2,1)}, bf16[768,1024]{1,0:T(8,128)(2,1)}, bf16[768...) custom-call(bf16[2,16,24,1024]{3,2,1,0:T(8,128)(2,1)} %tokens.1, ...), custom_call_target="tpu_custom_call" | custom-call | tf_op jit(solution)/shard_map/front/pallas_call | solution.py:666
  46.9 76.1 %back.1 = (f32[8,3072]{1,0:T(8,128)}, f32[8,1024]{1,0:T(8,128)}, bf16[2,16,24,1024]{3,2,1,0:T(8,128)(2,1)}, bf16[192,1024]{1,0:T(8,128)(2,1)}) custom-call(bf16[768,1024]{1,0:T(8,128)(2,1)} %get-tuple-element.18.q_hbm, bf16[768,1024]{1,0:T(8,128)(2,1)} %get-tuple-element.19.k_hbm, bf16[768,1024]{1,0:T(8,128)(2,1)} %get-tuple-element.20.v_hbm, ...), custom_call_target="tpu_custom_call" | custom-call | tf_op jit(solution)/shard_map/back/pallas_call | solution.py:442
  123.0 1.8 %copy.21 = bf16[2,8,12,1024]{3,1,2,0:T(8,128)(2,1)} copy(bf16[2,8,12,1024]{3,1,2,0:T(8,128)(2,1)} %bitcast.6) | data formatting | bytes 786432
  124.8 0.0 copy-start
  124.8 0.0 copy-start.1
  124.8 2.7 %copy.22 = bf16[2,16,24,1024]{3,2,1,0:T(8,128)(2,1)} copy(bf16[2,16,24,1024]{3,2,1,0:T(8,128)(2,1)} %get-tuple-element.37) | data formatting | bytes 3145728
  127.5 0.0 copy-done
  127.5 0.6 copy.23
  128.2 0.0 copy-done.1
  128.2 0.6 copy.24
Async XLA Ops:
  124.8 2.7 %copy-start = (f32[8,3072]{1,0:T(8,128)S(1)}, f32[8,3072]{1,0:T(8,128)}, u32[]{:S(2)}) copy-start(f32[8,3072]{1,0:T(8,128)} %get-tuple-element.38) | copy-start | bytes 294916
  124.8 3.4 %copy-start.1 = (f32[8,1024]{1,0:T(8,128)S(1)}, f32[8,1024]{1,0:T(8,128)}, u32[]{:S(2)}) copy-start(f32[8,1024]{1,0:T(8,128)} %get-tuple-element.39) | copy-start | bytes 98308
where the time goes:
time: 130 us; the launch traced here: 129 us
  Pallas kernels  122 us (94%)
  local copies, waits for them, and re-layouts  5.74 us (4%)
    pallas_call x1, Pallas kernels, back(): pl.pallas_call(back_kernel, out_shape=(jax.ShapeDtypeStruct((8, 3072), F3...  76.1 us
    pallas_call x1, Pallas kernels, front(): pl.pallas_call(front_kernel, out_shape=(rows, turned, rows, rows, rows, r...  46.2 us
    unnamed x8, local copies, waits for them, and re-layouts  5.74 us

commit v1 on v0

--- a/solution.py
+++ b/solution.py
@@ -7,6 +7,7 @@
 from jax.sharding import PartitionSpec as P
 
 CHUNKS = 4
+ROUTES = ((0, 1, 2), (1, 0, 2), (2, 1, 0), (0, 1, 2), (1, 0, 2))
 MESH = pl.DeviceIdType.MESH
 F32, BF16 = jnp.float32, jnp.bfloat16
 epsilon = 1e-05
@@ -170,7 +171,7 @@
     for copy in merged_copies:
         copy.start()
 
-    streams = ((g_x, 0), (g_y, 1), (g_z, 2), (g_p, 1), (g_r, 2))
+    streams = ((g_x, ROUTES[0]), (g_y, ROUTES[1]), (g_z, ROUTES[2]), (g_p, ROUTES[3]), (g_r, ROUTES[4]))
     buffers = tuple(stream_buffers[7 * i:7 * i + 7] for i in range(5))
 
     def slot_of(kind, chunk):
@@ -185,8 +186,8 @@
         into = buffers[kind][2 + 2 * level].at[chunk]
         dims = "hzyl"
         for i in range(level):
-            dims = left_over(dims, (streams[kind][1] + i) % 3)
-        return acc, into, dims, (streams[kind][1] + level) % 3
+            dims = left_over(dims, streams[kind][1][i])
+        return acc, into, dims, streams[kind][1][level]
 
     def level_copies(kind, chunk, level):
         acc, into, dims, axis = level_refs(kind, chunk, level)
@@ -239,7 +240,8 @@
         g = streams[kind][0]
         width = g.shape[-1]
         both = jnp.concatenate([terms[:, :, :width], terms[:, :, width:]], axis=1)
-        g[slot_of(kind, chunk), pl.ds(i * 16, 16)] = both.astype(BF16).reshape(16, 2, 16, width)
+        pairs = terms.shape[0] // 2
+        g[slot_of(kind, chunk), pl.ds(i * pairs, pairs)] = both.astype(BF16).reshape(pairs, 2, 16, width)
 
     def window_back(chunk, w):
         columns = pl.ds(pl.multiple_of(chunk * 256, 256), 256)
@@ -386,7 +388,7 @@
             normed_load.wait()
 
         for level in range(3):
-            @pl.when(t == level + 1)
+            @pl.when(t == level + 2)
             def _():
                 for kind in (3, 4):
                     level_to_next(kind, 0, level)
@@ -400,11 +402,11 @@
 
             columns = pl.ds(pl.multiple_of(t * 256, 256), 256)
 
-            @pl.loop(0, 4)
+            @pl.loop(0, 2)
             def _(i):
-                rows = pl.ds(pl.multiple_of(i * 256, 256), 256)
+                rows = pl.ds(pl.multiple_of(i * 512, 512), 512)
                 for kind, right in enumerate((dq, dk, dv)):
-                    put_terms(kind, t, i, dot(normed_turned[rows], right[:, columns]).reshape(32, 8, 256))
+                    put_terms(kind, t, i, dot(normed_turned[rows], right[:, columns]).reshape(64, 8, 256))
 
             for kind in range(3):
                 core_copy(kind, t).start()
@@ -431,9 +433,9 @@
 
 def back(q, k, v, mix, mix_grad, normed_turned, mix_turned, grad, x, qkv_weight, merged_groups):
     buffers = []
-    for axis, count, width in ((0, CHUNKS, 128), (1, CHUNKS, 128), (2, CHUNKS, 128), (1, 1, 256), (2, 1, 256)):
-        first = left_over("hzyl", axis)
-        second = left_over(first, (axis + 1) % 3)
+    for route, count, width in zip(ROUTES, (CHUNKS,) * 3 + (1,) * 2, (128,) * 3 + (256,) * 2):
+        first = left_over("hzyl", route[0])
+        second = left_over(first, route[1])
         for shape in ((64,), (2, 4, 4, 2), (3, *sizes(first)), sizes(first), (3, *sizes(second)), sizes(second), (3,)):
             buffers.append(pltpu.VMEM((count, *shape, 16, width), BF16))
     vmem, anywhere = pl.BlockSpec(memory_space=pltpu.VMEM), pl.BlockSpec(memory_space=pl.ANY)
@@ -485,7 +487,8 @@
 
     @pl.loop(0, 6)
     def _(i):
-        m, n = 1 - i // 3, i % 3
+        m = jnp.where((i >= 1) & (i <= 3), 1, 0)
+        n = jnp.where(i < 2, 2, 1 - i % 2)
         natural = [change[pl.ds(pl.multiple_of((level * 16 + 8 * m + row) * 24 + 8 * n, 8), 8)]
                    for level in range(2) for row in range(8)]
         quarters = dot(to_natural[...], jnp.concatenate(natural, axis=0).astype(BF16), TN)
@@ -494,14 +497,14 @@
             for side in range(2):
                 units[2 * m + 1 + u, 2 * n + 1 + side] = quarters[2 * u + side]
 
-        @pl.when(i == 2)
+        @pl.when(i == 1)
+        def _():
+            copies[1].start()
+
+        @pl.when(i == 3)
         def _():
             copies[0].start()
             copies[2].start()
-
-        @pl.when(i == 5)
-        def _():
-            copies[1].start()
 
     merged_in = dot(merged_natural[...], merged_grad[...], TN).reshape(4, 6, 8, 1024)
     for i in range(4):

time: 130 us -> 121 us (0.931)
  Pallas kernels: 122 us -> 113 us
    pallas_call x1, Pallas kernels: 76.1 us -> 62.9 us  [back(): pl.pallas_call(back_kernel, out_shape=(jax.ShapeDtypeStruct((8, 3072), F3...]
    pallas_call x1, Pallas kernels: 46.2 us -> 49.8 us  [front(): pl.pallas_call(front_kernel, out_shape=(rows, turned, rows, rows, rows, r...]
where the time goes in v1:
time: 121 us; the launch traced here: 119 us
  Pallas kernels  113 us (93%)
  local copies, waits for them, and re-layouts  5.74 us (5%)
    pallas_call x1, Pallas kernels, back(): pl.pallas_call(back_kernel, out_shape=(jax.ShapeDtypeStruct((8, 3072), F3...  62.9 us
    pallas_call x1, Pallas kernels, front(): pl.pallas_call(front_kernel, out_shape=(rows, turned, rows, rows, rows, r...  49.8 us
    unnamed x8, local copies, waits for them, and re-layouts  5.74 us

profile of v1, /device:TPU:1, one launch (start us, length us, event | category | flops | bytes accessed | tf_op | source)
XLA Modules:
  0.0 119.0 jit_solution(592249490857376687)
XLA Ops:
  0.6 49.8 %front.1 = (bf16[768,1024]{1,0:T(8,128)(2,1)}, bf16[1024,768]{1,0:T(8,128)(2,1)}, bf16[768,1024]{1,0:T(8,128)(2,1)}, bf16[768,1024]{1,0:T(8,128)(2,1)}, bf16[768...) custom-call(bf16[2,16,24,1024]{3,2,1,0:T(8,128)(2,1)} %tokens.1, ...), custom_call_target="tpu_custom_call" | custom-call | tf_op jit(solution)/shard_map/front/pallas_call | solution.py:669
  50.4 62.9 %back.1 = (f32[8,3072]{1,0:T(8,128)}, f32[8,1024]{1,0:T(8,128)}, bf16[2,16,24,1024]{3,2,1,0:T(8,128)(2,1)}, bf16[192,1024]{1,0:T(8,128)(2,1)}) custom-call(bf16[768,1024]{1,0:T(8,128)(2,1)} %get-tuple-element.18.q_hbm, bf16[768,1024]{1,0:T(8,128)(2,1)} %get-tuple-element.19.k_hbm, bf16[768,1024]{1,0:T(8,128)(2,1)} %get-tuple-element.20.v_hbm, ...), custom_call_target="tpu_custom_call" | custom-call | tf_op jit(solution)/shard_map/back/pallas_call | solution.py:444
  113.3 1.8 %copy.21 = bf16[2,8,12,1024]{3,1,2,0:T(8,128)(2,1)} copy(bf16[2,8,12,1024]{3,1,2,0:T(8,128)(2,1)} %bitcast.6) | data formatting | bytes 786432
  115.1 0.0 copy-start
  115.1 0.0 copy-start.1
  115.1 2.7 %copy.22 = bf16[2,16,24,1024]{3,2,1,0:T(8,128)(2,1)} copy(bf16[2,16,24,1024]{3,2,1,0:T(8,128)(2,1)} %get-tuple-element.37) | data formatting | bytes 3145728
  117.8 0.0 copy-done
  117.8 0.6 copy.23
  118.4 0.0 copy-done.1
  118.4 0.6 copy.24
Async XLA Ops:
  115.1 2.7 %copy-start = (f32[8,3072]{1,0:T(8,128)S(1)}, f32[8,3072]{1,0:T(8,128)}, u32[]{:S(2)}) copy-start(f32[8,3072]{1,0:T(8,128)} %get-tuple-element.38) | copy-start | bytes 294916
  115.1 3.4 %copy-start.1 = (f32[8,1024]{1,0:T(8,128)S(1)}, f32[8,1024]{1,0:T(8,128)}, u32[]{:S(2)}) copy-start(f32[8,1024]{1,0:T(8,128)} %get-tuple-element.39) | copy-start | bytes 98308

commit v2 on v1

--- a/solution.py
+++ b/solution.py
@@ -332,6 +332,16 @@
                                              + dot(dk[tokens], qkv_weight[rows, 1024:2048], NT)
                                              + dot(dv[tokens], qkv_weight[rows, 2048:3072], NT))
 
+            @pl.when(t == 4)
+            def _():
+                for kind in range(3):
+                    core_to_first(kind, 3)
+
+            @pl.when(t == 5)
+            def _():
+                for kind in range(3):
+                    level_to_next(kind, 3, 0)
+
             @pl.loop(0, 3)
             def _(wb):
                 finish_window((t - 4) * 3 + wb)
@@ -351,6 +361,8 @@
                 copy.wait_recv()
             framed = jnp.concatenate([merged_units[i, 1:7].reshape(48, 1024) for i in range(1, 5)], axis=0)
             merged_out[...] = dot(merged_natural[...], framed.astype(BF16)).astype(BF16)
+            for kind in range(3):
+                level_to_next(kind, 3, 1)
             strips[1].wait_recv()
 
         @pl.when(t == 7)
@@ -370,12 +382,12 @@
         for level in (2, 1, 0):
             chunk = t - 2 - level
 
-            @pl.when((chunk >= 0) & (chunk < CHUNKS))
+            @pl.when((chunk >= 0) & (chunk < CHUNKS - (level < 2)))
             def _():
                 for kind in range(3):
                     level_to_next(kind, chunk, level)
 
-        @pl.when((t >= 1) & (t <= CHUNKS))
+        @pl.when((t >= 1) & (t < CHUNKS))
         def _():
             for kind in range(3):
                 core_to_first(kind, t - 1)
@@ -470,7 +482,7 @@
                  to_natural, to_quarters, merged_natural, merged_windows,
                  x_hbm, normed_hbm, q_hbm, k_hbm, v_hbm, mix_hbm, mix_turned_hbm, grad_hbm, mix_grad_hbm, merged_out,
                  x, normed, normed_turned, q, k, v, mix, mix_turned, grad, mix_grad,
-                 qkv_weight, out_weight, merge_weight, scaled, change, inverses, groups, units, merged_units,
+                 qkv_weight, out_weight, merge_weight, merge_normed, scaled, change, inverses, groups, units, merged_units,
                  load, store, send, recv):
     loads = [pltpu.make_async_copy(source, target, load.at[i]) for i, (source, target) in enumerate(
         ((weight_hbm, qkv_weight), (out_weight_hbm, out_weight), (merge_weight_hbm, merge_weight)))]
@@ -553,57 +565,10 @@
              (mix_turned, mix_turned_hbm), (grad, grad_hbm), (mix_grad, mix_grad_hbm)]
     stores = [pltpu.make_async_copy(source, target, store.at[i]) for i, (source, target) in enumerate(keeps)]
 
-    @pl.loop(0, 2)
-    def _(phase):
-        half = 1 - phase
-
-        @pl.loop(0, 3)
-        def _(i):
-            @pl.when((phase == 0) & (i == 2))
-            def _():
-                copies[1].wait_recv()
-
-            @pl.when((phase == 1) & (i == 0))
-            def _():
-                copies[0].wait_recv()
-
-            @pl.when((phase == 1) & (i == 2))
-            def _():
-                copies[2].wait_recv()
-
-            window(half * 3 + (i + 1) % 3)
-
-        @pl.when(phase == 0)
-        def _():
-            loads[0].wait()
-
-        @pl.when(phase == 1)
-        def _():
-            stores[0].start()
-            stores[1].start()
-
-        project(half, 0)
-
-        @pl.loop(0, 3)
-        def _(chunk):
-            project(half, chunk + 1)
-            attend(half, chunk)
-
-        attend(half, 3)
-
-    for copy in stores[2:7]:
-        copy.start()
-    for copy in copies[3:]:
-        copy.wait_recv()
-    framed = jnp.concatenate([merged_units[i, 0:6].reshape(48, 1024) for i in range(4)], axis=0)
-    groups[...] = dot(merged_windows[...], framed.astype(BF16)).astype(BF16)
-    loads[1].wait()
-
-    def add_branch(chunk):
+    def add_branch(half, chunk):
+        rows = pl.ds(pl.multiple_of(half * 384, 384), 384)
         columns = pl.ds(pl.multiple_of(chunk * 256, 256), 256)
-        scaled[:, columns] = x[:, columns].astype(F32) + dot(mix[...], out_weight[:, columns])
-
-    pl.loop(0, 4)(add_branch)
+        scaled[rows, columns] = x[rows, columns].astype(F32) + dot(mix[rows], out_weight[:, columns])
 
     def quarter_rows(i):
         return [pl.ds(pl.multiple_of(i // 2 * 128 + j * 32 + i % 2 * 16, 16), 16) for j in range(4)]
@@ -619,18 +584,73 @@
         inverse = lax.rsqrt(spread + epsilon)
         inverses[pl.ds(pl.multiple_of(i * 16, 16), 16)] = jnp.broadcast_to(inverse, (16, 128))
         for part, rows in zip(parts, group_rows(i)):
-            normed[rows] = (part * inverse).astype(BF16)
+            merge_normed[rows] = (part * inverse).astype(BF16)
         for part, rows in zip(parts, quarter_rows(i)):
             scaled[rows] = part * inverse
 
-    pl.loop(0, 12)(normalize_groups)
+    @pl.loop(0, 2)
+    def _(phase):
+        half = 1 - phase
+
+        @pl.loop(0, 3)
+        def _(i):
+            @pl.when((phase == 0) & (i == 2))
+            def _():
+                copies[1].wait_recv()
+
+            @pl.when((phase == 1) & (i == 0))
+            def _():
+                copies[0].wait_recv()
+
+            @pl.when((phase == 1) & (i == 2))
+            def _():
+                copies[2].wait_recv()
+
+            window(half * 3 + (i + 1) % 3)
+
+        @pl.when(phase == 0)
+        def _():
+            loads[0].wait()
+
+        @pl.when(phase == 1)
+        def _():
+            stores[0].start()
+            stores[1].start()
+
+        project(half, 0)
+
+        @pl.loop(0, 3)
+        def _(chunk):
+            project(half, chunk + 1)
+            attend(half, chunk)
+
+        attend(half, 3)
+
+        @pl.when(phase == 0)
+        def _():
+            loads[1].wait()
+
+        @pl.loop(0, 4)
+        def _(chunk):
+            add_branch(half, chunk)
+
+        @pl.loop(0, 6)
+        def _(i):
+            normalize_groups(half * 6 + i)
+
+    for copy in stores[2:7]:
+        copy.start()
+    for copy in copies[3:]:
+        copy.wait_recv()
+    framed = jnp.concatenate([merged_units[i, 0:6].reshape(48, 1024) for i in range(4)], axis=0)
+    groups[...] = dot(merged_windows[...], framed.astype(BF16)).astype(BF16)
     loads[2].wait()
 
     def merge_columns(chunk):
         columns = pl.ds(pl.multiple_of(chunk * 256, 256), 256)
-        total = dot(normed[0:192], merge_weight[0:1024, columns])
+        total = dot(merge_normed[0:192], merge_weight[0:1024, columns])
         for j in range(1, 4):
-            total = total + dot(normed[192 * j:192 * j + 192], merge_weight[1024 * j:1024 * j + 1024, columns])
+            total = total + dot(merge_normed[192 * j:192 * j + 192], merge_weight[1024 * j:1024 * j + 1024, columns])
         merged_out[:, columns] = total.astype(BF16)
         for j in range(4):
             rows = pl.ds(pl.multiple_of(j * 1024 + chunk * 256, 256), 256)
@@ -674,7 +694,7 @@
         scratch_shapes=[
             rows_vmem, rows_vmem, turned_vmem, rows_vmem, rows_vmem, rows_vmem, rows_vmem, turned_vmem, rows_vmem,
             rows_vmem,
-            pltpu.VMEM((1024, 3072), BF16), pltpu.VMEM((1024, 1024), BF16), pltpu.VMEM((4096, 1024), BF16),
+            pltpu.VMEM((1024, 3072), BF16), pltpu.VMEM((1024, 1024), BF16), pltpu.VMEM((4096, 1024), BF16), rows_vmem,
             pltpu.VMEM((768, 1024), F32), pltpu.VMEM((768, 1024), F32), pltpu.VMEM((192, 128), F32),
             pltpu.VMEM((192, 1024), BF16),
             pltpu.VMEM((5, 7, 32, 1024), BF16),

time: 121 us -> 118 us (0.975)
  Pallas kernels: 113 us -> 110 us
    pallas_call x1, Pallas kernels: 49.8 us -> 47.5 us  [front(): pl.pallas_call(front_kernel, out_shape=(rows, turned, rows, rows, rows, r...]
where the time goes in v2:
time: 118 us; the launch traced here: 116 us
  Pallas kernels  110 us (93%)
  local copies, waits for them, and re-layouts  5.74 us (5%)
    pallas_call x1, Pallas kernels, back(): pl.pallas_call(back_kernel, out_shape=(jax.ShapeDtypeStruct((8, 3072), F3...  62.2 us
    pallas_call x1, Pallas kernels, front(): pl.pallas_call(front_kernel, out_shape=(rows, turned, rows, rows, rows, r...  47.5 us
    unnamed x8, local copies, waits for them, and re-layouts  5.74 us

profile of v2, /device:TPU:1, one launch (start us, length us, event | category | flops | bytes accessed | tf_op | source)
XLA Modules:
  0.0 116.1 jit_solution(9028347949988793161)
XLA Ops:
  0.6 47.5 %front.1 = (bf16[768,1024]{1,0:T(8,128)(2,1)}, bf16[1024,768]{1,0:T(8,128)(2,1)}, bf16[768,1024]{1,0:T(8,128)(2,1)}, bf16[768,1024]{1,0:T(8,128)(2,1)}, bf16[768...) custom-call(bf16[2,16,24,1024]{3,2,1,0:T(8,128)(2,1)} %tokens.1, ...), custom_call_target="tpu_custom_call" | custom-call | tf_op jit(solution)/shard_map/front/pallas_call | solution.py:689
  48.1 62.2 %back.1 = (f32[8,3072]{1,0:T(8,128)}, f32[8,1024]{1,0:T(8,128)}, bf16[2,16,24,1024]{3,2,1,0:T(8,128)(2,1)}, bf16[192,1024]{1,0:T(8,128)(2,1)}) custom-call(bf16[768,1024]{1,0:T(8,128)(2,1)} %get-tuple-element.18.q_hbm, bf16[768,1024]{1,0:T(8,128)(2,1)} %get-tuple-element.19.k_hbm, bf16[768,1024]{1,0:T(8,128)(2,1)} %get-tuple-element.20.v_hbm, ...), custom_call_target="tpu_custom_call" | custom-call | tf_op jit(solution)/shard_map/back/pallas_call | solution.py:456
  110.4 1.8 %copy.21 = bf16[2,8,12,1024]{3,1,2,0:T(8,128)(2,1)} copy(bf16[2,8,12,1024]{3,1,2,0:T(8,128)(2,1)} %bitcast.6) | data formatting | bytes 786432
  112.1 0.0 copy-start
  112.1 0.0 copy-start.1
  112.1 2.7 %copy.22 = bf16[2,16,24,1024]{3,2,1,0:T(8,128)(2,1)} copy(bf16[2,16,24,1024]{3,2,1,0:T(8,128)(2,1)} %get-tuple-element.37) | data formatting | bytes 3145728
  114.9 0.0 copy-done
  114.9 0.6 copy.23
  115.5 0.0 copy-done.1
  115.5 0.6 copy.24
Async XLA Ops:
  112.1 2.7 %copy-start = (f32[8,3072]{1,0:T(8,128)S(1)}, f32[8,3072]{1,0:T(8,128)}, u32[]{:S(2)}) copy-start(f32[8,3072]{1,0:T(8,128)} %get-tuple-element.38) | copy-start | bytes 294916
  112.1 3.4 %copy-start.1 = (f32[8,1024]{1,0:T(8,128)S(1)}, f32[8,1024]{1,0:T(8,128)}, u32[]{:S(2)}) copy-start(f32[8,1024]{1,0:T(8,128)} %get-tuple-element.39) | copy-start | bytes 98308

commit v3 on v2

--- a/solution.py
+++ b/solution.py
@@ -67,11 +67,14 @@
     return (lat_there, lon), (lat, lon_there), (lat_there, lon_there)
 
 
-def greet(receive_from, send_to):
+def greet(receive_from):
     barrier = pltpu.get_barrier_semaphore()
     for device in receive_from:
         pl.semaphore_signal(barrier, inc=1, device_id=device, device_id_type=MESH)
-    pl.semaphore_wait(barrier, len(send_to))
+
+
+def await_greetings(send_to):
+    pl.semaphore_wait(pltpu.get_barrier_semaphore(), len(send_to))
 
 
 def remote(source, target, send, recv, device):
@@ -137,10 +140,10 @@
 
     normed_load, mix_load = fetch(20, normed_hbm, normed_turned), fetch(21, mix_turned_hbm, mix_turned)
     grad_load, weight_load, x_load = fetch(22, grad_hbm, grad), fetch(23, weight_hbm, qkv_weight), fetch(24, x_hbm, x_in)
+    for copy in chunk_loads(0):
+        copy.start()
     mix_load.start()
     grad_load.start()
-    for copy in chunk_loads(0):
-        copy.start()
     normed_load.start()
 
     @pl.loop(1, CHUNKS)
@@ -162,15 +165,12 @@
     sibling = device_at(x, y, z, 1 - core)
     ring = [sibling] + [moved(axis, step) for axis in range(3) for step in (1, 2, 3)]
     before, after = neighbours(-1), neighbours(1)
-    greet(ring + list(after), ring + list(before))
+    greet(ring + list(after))
 
     units_in = dot(merged_windows[...], merged_in[...], TN).reshape(4, 6, 8, 1024)
     for i in range(4):
         merged_units[i, 0:6] = units_in[i]
     merged_copies = frame_copies(merged_units, (0, 0), (4, 6), strip_send, strip_recv, 0, before)
-    for copy in merged_copies:
-        copy.start()
-
     streams = ((g_x, ROUTES[0]), (g_y, ROUTES[1]), (g_z, ROUTES[2]), (g_p, ROUTES[3]), (g_r, ROUTES[4]))
     buffers = tuple(stream_buffers[7 * i:7 * i + 7] for i in range(5))
 
@@ -272,19 +272,6 @@
                 pieces.append(dot(turned[low:low + 32], scores_grad[head][:, group * 128:group * 128 + 128]))
         dq[rows, columns] = (jnp.concatenate(pieces, axis=0).T * SCALE).astype(BF16)
 
-    mix_load.wait()
-    grad_load.wait()
-
-    @pl.loop(0, 4)
-    def _(i):
-        rows = pl.ds(pl.multiple_of(i * 256, 256), 256)
-        for kind in (3, 4):
-            low = (kind - 3) * 512
-            put_terms(kind, 0, i, dot(mix_turned[rows], grad[:, low:low + 512]).reshape(32, 8, 512))
-
-    for kind in (3, 4):
-        core_copy(kind, 0).start()
-
     def finish_window(w):
         pieces = []
         for i in range(4):
@@ -316,6 +303,26 @@
                 for wb in range(3):
                     window_back(t, wa * 3 + wb)
 
+        @pl.when(t == 0)
+        def _():
+            await_greetings(ring + list(before))
+            for copy in merged_copies:
+                copy.start()
+            mix_load.wait()
+            grad_load.wait()
+
+            @pl.loop(0, 4)
+            def _(i):
+                rows = pl.ds(pl.multiple_of(i * 256, 256), 256)
+                for kind in (3, 4):
+                    low = (kind - 3) * 512
+                    put_terms(kind, 0, i, dot(mix_turned[rows], grad[:, low:low + 512]).reshape(32, 8, 512))
+
+            for kind in (3, 4):
+                core_copy(kind, 0).start()
+
+            normed_load.wait()
+
         @pl.when((t == 4) | (t == 5))
         def _():
             @pl.when(t == 4)
@@ -392,15 +399,13 @@
             for kind in range(3):
                 core_to_first(kind, t - 1)
 
-        @pl.when(t == 0)
+        @pl.when(t == 1)
         def _():
             for kind in (3, 4):
                 core_to_first(kind, 0)
 
-            normed_load.wait()
-
         for level in range(3):
-            @pl.when(t == level + 2)
+            @pl.when(t == level + 3)
             def _():
                 for kind in (3, 4):
                     level_to_next(kind, 0, level)
@@ -478,6 +483,30 @@
     )(q, k, v, mix, mix_grad, normed_turned, mix_turned, grad, x, qkv_weight, merged_groups, *orders())
 
 
+def place_kernel(tokens, merged, qkv, out, tokens_out, merged_out, qkv_out, out_out, done):
+    copies = [pltpu.make_async_copy(tokens.at[i // 2, pl.ds(i % 2 * 8, 8)], tokens_out.at[i // 2, pl.ds(i % 2 * 8, 8)],
+                                    done.at[i]) for i in range(4)]
+    copies += [pltpu.make_async_copy(merged, merged_out, done.at[4]), pltpu.make_async_copy(qkv, qkv_out, done.at[5]),
+               pltpu.make_async_copy(out, out_out, done.at[6])]
+    for copy in copies:
+        copy.start()
+    for copy in copies:
+        copy.wait()
+
+
+def place_results(*results):
+    anywhere = pl.BlockSpec(memory_space=pl.ANY)
+    return pl.pallas_call(
+        place_kernel,
+        out_shape=tuple(jax.ShapeDtypeStruct(result.shape, result.dtype) for result in results),
+        in_specs=[anywhere] * 4,
+        out_specs=(anywhere,) * 4,
+        scratch_shapes=[pltpu.SemaphoreType.DMA((7,))],
+        compiler_params=pltpu.CompilerParams(vmem_limit_bytes=62 * MIB),
+        name="place_results",
+    )(*results)
+
+
 def front_kernel(tokens, merged_grad, weight_hbm, out_weight_hbm, merge_weight_hbm,
                  to_natural, to_quarters, merged_natural, merged_windows,
                  x_hbm, normed_hbm, q_hbm, k_hbm, v_hbm, mix_hbm, mix_turned_hbm, grad_hbm, mix_grad_hbm, merged_out,
@@ -489,13 +518,15 @@
     for copy in loads:
         copy.start()
     before, after = neighbours(-1), neighbours(1)
-    greet(before, after)
+    greet(before)
     copies = (frame_copies(units, (4, 6), (0, 0), send, recv, 0, after)
               + frame_copies(merged_units, (4, 6), (0, 0), send, recv, 3, after))
 
     @pl.loop(0, 32)
     def _(i):
         change[pl.ds(pl.multiple_of(i * 24, 8), 24)] = tokens[i // 16, i % 16].astype(F32)
+
+    await_greetings(after)
 
     @pl.loop(0, 6)
     def _(i):
@@ -714,6 +745,8 @@
         tokens, merged_grad.transpose(0, 2, 1, 3).reshape(192, 1024), qkv_weight, out_weight, merge_weight)
     qkv_weight_grad, out_weight_grad, tokens_grad, merged = back(
         q, k, v, mixture, mixture_grad, normed_turned, mix_turned, grad, x, qkv_weight, merged_groups)
+    tokens_grad, merged, qkv_weight_grad, out_weight_grad = place_results(
+        tokens_grad, merged, qkv_weight_grad, out_weight_grad)
     merged = merged.reshape(2, 12, 8, 1024).transpose(0, 2, 1, 3)
     return (merged, tokens_grad, qkv_weight_grad, out_weight_grad)
 

time: 118 us -> 174 us (1.47)
  Pallas kernels: 110 us -> 172 us
  local copies, waits for them, and re-layouts: 5.74 us -> 0 us
    pallas_call x0 -> x1, Pallas kernels: none -> 64.7 us  [place_results(): pl.pallas_call(place_kernel, out_shape=tuple((jax.ShapeDtypeStruct(result...]
    unnamed x8 -> x0, local copies, waits for them, and re-layouts: 5.74 us -> none
    pallas_call x1, Pallas kernels: 62.2 us -> 60.3 us  [back(): pl.pallas_call(back_kernel, out_shape=(jax.ShapeDtypeStruct((8, 3072), F3...]
where the time goes in v3:
time: 174 us; the launch traced here: 172 us
  Pallas kernels  172 us (99%)
    pallas_call x1, Pallas kernels, place_results(): pl.pallas_call(place_kernel, out_shape=tuple((jax.ShapeDtypeStruct(result...  64.7 us
    pallas_call x1, Pallas kernels, back(): pl.pallas_call(back_kernel, out_shape=(jax.ShapeDtypeStruct((8, 3072), F3...  60.3 us
    pallas_call x1, Pallas kernels, front(): pl.pallas_call(front_kernel, out_shape=(rows, turned, rows, rows, rows, r...  46.6 us

profile of v3, /device:TPU:1, one launch (start us, length us, event | category | flops | bytes accessed | tf_op | source)
XLA Modules:
  0.0 172.3 jit_solution(14674045582800542388)
XLA Ops:
  0.6 46.6 %front.1 = (bf16[768,1024]{1,0:T(8,128)(2,1)}, bf16[1024,768]{1,0:T(8,128)(2,1)}, bf16[768,1024]{1,0:T(8,128)(2,1)}, bf16[768,1024]{1,0:T(8,128)(2,1)}, bf16[768...) custom-call(bf16[2,16,24,1024]{3,2,1,0:T(8,128)(2,1)} %tokens.1, ...), custom_call_target="tpu_custom_call" | custom-call | tf_op jit(solution)/shard_map/front/pallas_call | solution.py:720
  47.3 60.3 %back.1 = (f32[8,3072]{1,0:T(8,128)}, f32[8,1024]{1,0:T(8,128)}, bf16[2,16,24,1024]{3,2,1,0:T(8,128)(2,1)}, bf16[192,1024]{1,0:T(8,128)(2,1)}) custom-call(bf16[768,1024]{1,0:T(8,128)(2,1)} %get-tuple-element.22.q_hbm, bf16[768,1024]{1,0:T(8,128)(2,1)} %get-tuple-element.23.k_hbm, bf16[768,1024]{1,0:T(8,128)(2,1)} %get-tuple-element.24.v_hbm, ...), custom_call_target="tpu_custom_call" | custom-call | tf_op jit(solution)/shard_map/back/pallas_call | solution.py:461
  107.6 64.7 %place_results.1 = (bf16[2,16,24,1024]{3,2,1,0:T(8,128)(2,1)}, bf16[192,1024]{1,0:T(8,128)(2,1)}, f32[8,3072]{1,0:T(8,128)}, f32[8,1024]{1,0:T(8,128)}) custom-call(bf16[2,16,24,1024]{3,2,1,0:T(8,128)(2,1)} %get-tuple-element.32.tokens, bf16[192,1024]{1,0:T(8,128)(2,1)} %get-tuple-element.33.merged, f32[8,3072]{1,0:T(8,128)} %get-tuple-element.34.qkv, ...), custom_call_target="tpu_custom_call" | custom-call | tf_op jit(solution)/shard_map/place_results/pallas_call | solution.py:499

commit v4 on v3

--- a/solution.py
+++ b/solution.py
@@ -483,25 +483,22 @@
     )(q, k, v, mix, mix_grad, normed_turned, mix_turned, grad, x, qkv_weight, merged_groups, *orders())
 
 
-def place_kernel(tokens, merged, qkv, out, tokens_out, merged_out, qkv_out, out_out, done):
-    copies = [pltpu.make_async_copy(tokens.at[i // 2, pl.ds(i % 2 * 8, 8)], tokens_out.at[i // 2, pl.ds(i % 2 * 8, 8)],
-                                    done.at[i]) for i in range(4)]
-    copies += [pltpu.make_async_copy(merged, merged_out, done.at[4]), pltpu.make_async_copy(qkv, qkv_out, done.at[5]),
-               pltpu.make_async_copy(out, out_out, done.at[6])]
-    for copy in copies:
-        copy.start()
-    for copy in copies:
-        copy.wait()
+def place_kernel(tokens, merged, qkv, out, tokens_out, merged_out, qkv_out, out_out):
+    tokens_out[...] = tokens[...]
+    merged_out[...] = merged[...]
+    qkv_out[...] = qkv[...]
+    out_out[...] = out[...]
 
 
 def place_results(*results):
-    anywhere = pl.BlockSpec(memory_space=pl.ANY)
+    blocks = (pl.BlockSpec((1, 8, 24, 1024), lambda i: (i // 2, i % 2, 0, 0)), pl.BlockSpec((48, 1024), lambda i: (i, 0)),
+              pl.BlockSpec((8, 768), lambda i: (0, i)), pl.BlockSpec((8, 256), lambda i: (0, i)))
     return pl.pallas_call(
         place_kernel,
+        grid=(4,),
         out_shape=tuple(jax.ShapeDtypeStruct(result.shape, result.dtype) for result in results),
-        in_specs=[anywhere] * 4,
-        out_specs=(anywhere,) * 4,
-        scratch_shapes=[pltpu.SemaphoreType.DMA((7,))],
+        in_specs=list(blocks),
+        out_specs=blocks,
         compiler_params=pltpu.CompilerParams(vmem_limit_bytes=62 * MIB),
         name="place_results",
     )(*results)

time: 174 us -> 113 us (0.65)
  Pallas kernels: 172 us -> 111 us
    pallas_call x1, Pallas kernels: 64.7 us -> 3.78 us  [place_results(): pl.pallas_call(place_kernel, grid=(4,), out_shape=tuple((jax.ShapeDtypeSt...]
where the time goes in v4:
time: 113 us; the launch traced here: 111 us
  Pallas kernels  111 us (98%)
    pallas_call x1, Pallas kernels, back(): pl.pallas_call(back_kernel, out_shape=(jax.ShapeDtypeStruct((8, 3072), F3...  60.3 us
    pallas_call x1, Pallas kernels, front(): pl.pallas_call(front_kernel, out_shape=(rows, turned, rows, rows, rows, r...  46.6 us
    pallas_call x1, Pallas kernels, place_results(): pl.pallas_call(place_kernel, grid=(4,), out_shape=tuple((jax.ShapeDtypeSt...  3.78 us

profile of v4, /device:TPU:1, one launch (start us, length us, event | category | flops | bytes accessed | tf_op | source)
XLA Modules:
  0.0 111.4 jit_solution(14497653849029061605)
XLA Ops:
  0.6 46.6 %front.1 = (bf16[768,1024]{1,0:T(8,128)(2,1)}, bf16[1024,768]{1,0:T(8,128)(2,1)}, bf16[768,1024]{1,0:T(8,128)(2,1)}, bf16[768,1024]{1,0:T(8,128)(2,1)}, bf16[768...) custom-call(bf16[2,16,24,1024]{3,2,1,0:T(8,128)(2,1)} %tokens.1, ...), custom_call_target="tpu_custom_call" | custom-call | tf_op jit(solution)/shard_map/front/pallas_call | solution.py:717
  47.3 60.3 %back.1 = (f32[8,3072]{1,0:T(8,128)}, f32[8,1024]{1,0:T(8,128)}, bf16[2,16,24,1024]{3,2,1,0:T(8,128)(2,1)}, bf16[192,1024]{1,0:T(8,128)(2,1)}) custom-call(bf16[768,1024]{1,0:T(8,128)(2,1)} %get-tuple-element.22.q_hbm, bf16[768,1024]{1,0:T(8,128)(2,1)} %get-tuple-element.23.k_hbm, bf16[768,1024]{1,0:T(8,128)(2,1)} %get-tuple-element.24.v_hbm, ...), custom_call_target="tpu_custom_call" | custom-call | tf_op jit(solution)/shard_map/back/pallas_call | solution.py:461
  107.6 3.8 %place_results.1 = (bf16[2,16,24,1024]{3,2,1,0:T(8,128)(2,1)}, bf16[192,1024]{1,0:T(8,128)(2,1)}, f32[8,3072]{1,0:T(8,128)}, f32[8,1024]{1,0:T(8,128)}) custom-call(bf16[2,16,24,1024]{3,2,1,0:T(8,128)(2,1)} %get-tuple-element.32.tokens, bf16[192,1024]{1,0:T(8,128)(2,1)} %get-tuple-element.33.merged, f32[8,3072]{1,0:T(8,128)} %get-tuple-element.34.qkv, ...), custom_call_target="tpu_custom_call" | custom-call | tf_op jit(solution)/shard_map/place_results/pallas_call | solution.py:496

commit v5 on v4

--- a/solution.py
+++ b/solution.py
@@ -12,6 +12,7 @@
 F32, BF16 = jnp.float32, jnp.bfloat16
 epsilon = 1e-05
 SCALE = 32 ** -0.5
+SCALE2 = SCALE * 1.4426950408889634
 MIB = 1024 * 1024
 NT = (((1,), (1,)), ((), ()))
 TN = (((0,), (0,)), ((), ()))
@@ -250,7 +251,7 @@
         out_grad = mix_grad[rows, columns]
         product = (out_grad.astype(F32) * mix[rows, columns].astype(F32)).astype(BF16)
         spread_queries, spread_grads = stack(queries, group_mask), stack(out_grad, group_mask)
-        weights = jnp.exp(dot(stack(keys, head_mask), spread_queries, NT) * SCALE)
+        weights = jnp.exp2(dot(stack(keys, head_mask), spread_queries, NT) * SCALE2)
         weights = jnp.where(other_region(512, 256, edge & (w < 3)), 0.0, weights)
         change = dot(stack(values, head_mask), spread_grads, NT)
         means = dot(own_head, product, NT)
@@ -419,13 +420,12 @@
 
             columns = pl.ds(pl.multiple_of(t * 256, 256), 256)
 
-            @pl.loop(0, 2)
-            def _(i):
-                rows = pl.ds(pl.multiple_of(i * 512, 512), 512)
-                for kind, right in enumerate((dq, dk, dv)):
+            for kind, right in enumerate((dq, dk, dv)):
+                @pl.loop(0, 2)
+                def _(i):
+                    rows = pl.ds(pl.multiple_of(i * 512, 512), 512)
                     put_terms(kind, t, i, dot(normed_turned[rows], right[:, columns]).reshape(64, 8, 256))
 
-            for kind in range(3):
                 core_copy(kind, t).start()
 
     for kind in range(3):
@@ -578,7 +578,7 @@
         for wb in range(3):
             rows = pl.ds(pl.multiple_of(half * 384 + wb * 128, 128), 128)
             scores = dot(stack(q[rows, columns], head_mask), stack(k[rows, columns], group_mask), NT)
-            weights = jnp.exp(scores * SCALE)
+            weights = jnp.exp2(scores * SCALE2)
             weights = jnp.where(other_region(512, 256, edge & (half == 0)), 0.0, weights)
             pieces = []
             for group in range(2):

time: 113 us -> 115 us (1.018)
    pallas_call x1, Pallas kernels: 60.3 us -> 62 us  [back(): pl.pallas_call(back_kernel, out_shape=(jax.ShapeDtypeStruct((8, 3072), F3...]
where the time goes in v5:
time: 115 us; the launch traced here: 113 us
  Pallas kernels  112 us (97%)
    pallas_call x1, Pallas kernels, back(): pl.pallas_call(back_kernel, out_shape=(jax.ShapeDtypeStruct((8, 3072), F3...  62 us
    pallas_call x1, Pallas kernels, front(): pl.pallas_call(front_kernel, out_shape=(rows, turned, rows, rows, rows, r...  46.6 us
    pallas_call x1, Pallas kernels, place_results(): pl.pallas_call(place_kernel, grid=(4,), out_shape=tuple((jax.ShapeDtypeSt...  3.78 us

profile of v5, /device:TPU:1, one launch (start us, length us, event | category | flops | bytes accessed | tf_op | source)
XLA Modules:
  0.0 113.0 jit_solution(9511893081491845113)
XLA Ops:
  0.6 46.6 %front.1 = (bf16[768,1024]{1,0:T(8,128)(2,1)}, bf16[1024,768]{1,0:T(8,128)(2,1)}, bf16[768,1024]{1,0:T(8,128)(2,1)}, bf16[768,1024]{1,0:T(8,128)(2,1)}, bf16[768...) custom-call(bf16[2,16,24,1024]{3,2,1,0:T(8,128)(2,1)} %tokens.1, ...), custom_call_target="tpu_custom_call" | custom-call | tf_op jit(solution)/shard_map/front/pallas_call | solution.py:717
  47.2 62.0 %back.1 = (f32[8,3072]{1,0:T(8,128)}, f32[8,1024]{1,0:T(8,128)}, bf16[2,16,24,1024]{3,2,1,0:T(8,128)(2,1)}, bf16[192,1024]{1,0:T(8,128)(2,1)}) custom-call(bf16[768,1024]{1,0:T(8,128)(2,1)} %get-tuple-element.22.q_hbm, bf16[768,1024]{1,0:T(8,128)(2,1)} %get-tuple-element.23.k_hbm, bf16[768,1024]{1,0:T(8,128)(2,1)} %get-tuple-element.24.v_hbm, ...), custom_call_target="tpu_custom_call" | custom-call | tf_op jit(solution)/shard_map/back/pallas_call | solution.py:461
  109.2 3.8 %place_results.1 = (bf16[2,16,24,1024]{3,2,1,0:T(8,128)(2,1)}, bf16[192,1024]{1,0:T(8,128)(2,1)}, f32[8,3072]{1,0:T(8,128)}, f32[8,1024]{1,0:T(8,128)}) custom-call(bf16[2,16,24,1024]{3,2,1,0:T(8,128)(2,1)} %get-tuple-element.32.tokens, bf16[192,1024]{1,0:T(8,128)(2,1)} %get-tuple-element.33.merged, f32[8,3072]{1,0:T(8,128)} %get-tuple-element.34.qkv, ...), custom_call_target="tpu_custom_call" | custom-call | tf_op jit(solution)/shard_map/place_results/pallas_call | solution.py:496
